TPU v7x, 32 devices: a whole 2x2x4 slice. The times are simulated.
32 devices in a mesh: groups: 2 (over y), vocab: 8 (over z, x), tok: 2 (over core).
Axes of the slice: x: 2, y: 2, z: 4, core: 2. Of those that a mesh axis runs over, the one named last changes fastest.
Arguments:
- hid_student: bfloat16 [32, 4096], P(('groups', 'vocab', 'tok')), parts along dimension 0, may hold values from -170 to 170
- teacher_logits: float32 [32, 8192], P(('groups', 'vocab', 'tok')), parts along dimension 0, may hold values from -288 to 288
- token_scale: bfloat16 [32], P(('groups', 'vocab', 'tok')), parts along dimension 0, may hold values from 128 to 1024
- head_student: bfloat16 [4096, 8192], P('tok', 'vocab'), may hold values from -0.09375 to 0.09375
Outputs:
- divergence: float32 [32], P(('groups', 'vocab', 'tok')), parts along dimension 0
- grad_hidden: bfloat16 [32, 4096], P(('groups', 'vocab', 'tok')), parts along dimension 0
There are 2 independent parts, one for each index of `groups`. A program takes and returns all parts, laid end to end along the dimension named above; an argument that names none is the same for every part. Nothing has to cross between parts.
All inputs are finite; a program needn't handle non-finite values.
Results may differ from a plain program's by a relative error of at most 0.0049.
Values may be sent and summed in bfloat16 or wider, within the bound.
A program may use at most 64 MiB of HBM per device.

v0:
```python
import jax
import jax.numpy as jnp
from jax import lax
from jax.sharding import PartitionSpec as P


def normalizers(student, teacher):
    peak_s = jnp.max(student, axis=1)
    peak_t = jnp.max(teacher, axis=1)
    top_s, top_t = lax.pmax((peak_s, peak_t), "vocab")
    local_s = jnp.sum(jnp.exp(student - top_s[:, None]), axis=1)
    local_t = jnp.sum(jnp.exp(teacher - top_t[:, None]), axis=1)
    mass_s, mass_t = lax.psum((local_s, local_t), "vocab")
    return (top_s + jnp.log(mass_s), top_t + jnp.log(mass_t))


def divergence_rows(student, teacher, scales):
    norm_s, norm_t = normalizers(student, teacher)
    logp = student - norm_s[:, None]
    logq = teacher - norm_t[:, None]
    logm = jnp.logaddexp(logp, logq) + jnp.log(jnp.float32(0.5))
    prob_p = jnp.exp(logp)
    prob_q = jnp.exp(logq)
    part_p = jnp.sum(prob_p * (logp - logm), axis=1)
    part_q = jnp.sum(prob_q * (logq - logm), axis=1)
    kl_p, kl_q = lax.psum((part_p, part_q), "vocab")
    loss_rows = 0.5 * kl_p + 0.5 * kl_q
    weights = scales.astype(jnp.float32)[:, None]
    grad_logits = (weights * prob_p * 0.5 * (logp - logm - kl_p[:, None])).astype(jnp.bfloat16)
    return (loss_rows, grad_logits)


def local(hid_student, teacher_logits, token_scale, head_student):
    rows = hid_student.shape[0]
    vocab_pos = lax.axis_index("vocab")
    teacher = lax.all_to_all(teacher_logits, "vocab", split_axis=1, concat_axis=0, tiled=True)
    full_s = lax.all_gather(head_student, "tok", axis=0, tiled=True)
    all_s, scales = (
        lax.all_gather(hid_student, "vocab", axis=0, tiled=True),
        lax.all_gather(token_scale, "vocab", axis=0, tiled=True),
    )
    student = jnp.dot(all_s, full_s, preferred_element_type=jnp.float32)
    loss_rows, grad_logits = divergence_rows(student, teacher, scales)
    grad_rows = lax.psum_scatter(
        lax.dot_general(
            grad_logits, full_s, (((1,), (1,)), ((), ())), preferred_element_type=jnp.float32
        ),
        "vocab",
        scatter_dimension=0,
        tiled=True,
    ).astype(jnp.bfloat16)
    loss_own = lax.dynamic_slice_in_dim(loss_rows, vocab_pos * rows, rows, 0)
    return (loss_own, grad_rows)


def solution(mesh):
    in_specs = (
        P(("groups", "vocab", "tok"), None),
        P(("groups", "vocab", "tok"), None),
        P(("groups", "vocab", "tok")),
        P("tok", "vocab"),
    )
    out_specs = (P(("groups", "vocab", "tok")), P(("groups", "vocab", "tok"), None))
    return jax.shard_map(local, mesh=mesh, in_specs=in_specs, out_specs=out_specs, check_vma=False)
```

profile of v0, /device:TPU:0, one launch (start us, length us, event | category | flops | bytes accessed | tf_op | source)
XLA Modules:
  0.0 180.2 jit_solution(17084674846332175499)
XLA Ops:
  7.2 0.0 all-gather.3.cloned.1.call-start
  7.2 0.7 all-gather.3.cloned.1.call-update
  7.9 7.3 %all-to-all-start = ((f32[1,8,1024]{2,0,1:T(1,128)}), f32[1,8,1024]{2,0,1:T(1,128)S(1)}, u32[]{:S(2)}, u32[]{:S(2)}) async-start(f32[1,8,1024]{2,0,1:T(1,128)} %bitcast.27), calls=%async_computation | async-start | bytes 65536 | tf_op jit(solution)/shard_map/all_to_all | solution.py:36
  15.8 1.3 fusion.18
  17.2 0.8 dynamic-update-slice
  17.9 21.8 %all-reduce = bf16[8]{0:T(256)(128)(2,1)S(1)} all-reduce(bf16[8]{0:T(256)(128)(2,1)S(1)} %dynamic-update-slice), channel_id=1, replica_groups=mesh['groups'=2,'vocab'=8,'tok'=2] {'vocab'}, use_global_device_ids=true, to_apply=%add | all-reduce | flops 8 | bytes 32
  39.8 30.7 %all-gather = bf16[8,1,4096]{2,1,0:T(2,128)(2,1)S(1)} all-gather(bf16[1,1,4096]{2,1,0:T(2,128)(2,1)} %bitcast.28), channel_id=1, replica_groups=mesh['groups'=2,'vocab'=8,'tok'=2] {'vocab'}, dimensions={0}, use_global_device_ids=true | all-gather | bytes 73728 | tf_op jit(solution)/shard_map/all_gather | solution.py:39
  70.5 0.0 all-to-all-done
  70.5 0.2 reduce_max.19
  70.6 0.0 all-gather.3.cloned.1.call-done
  70.7 4.7 %fusion.19 = (f32[8]{0:T(128)S(1)}, f32[8,1024]{1,0:T(8,128)S(1)}) fusion(bf16[4096,1024]{1,0:T(8,128)(2,1)} %all-gather.3.cloned.1.call-done, bf16[8,1,4096]{2,1,0:T(2,128)(2,1)S(1)} %all-gather), kind=kOutput, calls=%fused_computation.31 | convolution fusion | flops 67117048 | bytes 8486944 | tf_op jit(solution)/shard_map/dot_general | solution.py:42
  75.3 17.2 %all-reduce.4 = (f32[8]{0:T(128)S(1)}, f32[8]{0:T(128)S(1)}) all-reduce(f32[8]{0:T(128)S(1)} %reduce_max.19, f32[8]{0:T(128)S(1)} %get-tuple-element.12), channel_id=1, replica_groups=mesh['groups'=2,'vocab'=8,'tok'=2] {'vocab'}, use_global_device_ids=true, to_apply=%region_5.0 | all-reduce | flops 16 | bytes 128 | tf_op jit(solution)/shard_map/pmax | solution.py:10
  92.6 0.2 fusion.4
  92.8 19.0 %all-reduce.3 = (f32[8]{0:T(128)S(1)}, f32[8]{0:T(128)S(1)}) all-reduce(f32[8]{0:T(128)S(1)} %get-tuple-element.14, f32[8]{0:T(128)S(1)} %get-tuple-element.15), channel_id=1, replica_groups=mesh['groups'=2,'vocab'=8,'tok'=2] {'vocab'}, use_global_device_ids=true, to_apply=%region_7.0 | all-reduce | flops 16 | bytes 128 | tf_op jit(solution)/shard_map/psum | solution.py:13
  111.8 0.3 multiply_reduce_fusion
  112.1 17.3 %psum.30 = f32[8]{0:T(128)S(1)} all-reduce(f32[8]{0:T(128)S(1)} %get-tuple-element.3), channel_id=1, replica_groups=mesh['groups'=2,'vocab'=8,'tok'=2] {'vocab'}, use_global_device_ids=true, to_apply=%region_9.0 | all-reduce | flops 8 | bytes 64 | tf_op jit(solution)/shard_map/psum | solution.py:26
  129.4 5.7 %fusion.9 = f32[8,4096]{1,0:T(8,128)S(1)} fusion(bf16[4096,1024]{1,0:T(8,128)(2,1)} %all-gather.3.cloned.1.call-done, f32[8,1024]{1,0:T(8,128)S(1)} %get-tuple-element.13, f32[1,8,1024]{2,0,1:T(1,128)S(1)} %all-to-all-done, f32[8]{0:T(128)S(1)} %psum.30, f32[8]{0:T(128)S(1)} %convert_element_type.9, f32[8]{0:T(128)S(1)} %log_add_fusion, f32[8]{0:T(128)S(1)} %log_add_fusion.1), kind=kOutput, calls=%fused_computation.17 | convolution fusion | flops 67248128 | bytes 8585344 | tf_op jit(solution)/shard_map/dot_general | solution.py:45
  135.1 36.4 %all-reduce.6 = (f32[8]{0:T(128)S(1)}, bf16[8,4096]{1,0:T(8,128)(2,1)S(1)}) all-reduce(f32[8]{0:T(128)S(1)} %get-tuple-element.2, f32[8,4096]{1,0:T(8,128)S(1)} %fusion.9), channel_id=1, replica_groups=mesh['groups'=2,'vocab'=8,'tok'=2] {'vocab'}, use_global_device_ids=true, to_apply=%region_11.0 | all-reduce | flops 32776 | bytes 196672 | tf_op jit(solution)/shard_map/psum | solution.py:26
  171.5 0.6 dynamic_slice.3
  172.1 1.2 dynamic-slice_convert_fusion
  (5 shorter events, 0.0 us)
Async XLA Ops:
  7.2 63.5 %all-gather.3.cloned.1.call-start = ((), (), s32[]{:S(2)}) async-start(), calls=%async_computation.1 | async-start | bytes 12582912 | tf_op jit(solution)/shard_map/all_gather | solution.py:37
  7.9 62.6 %all-to-all-start = ((f32[1,8,1024]{2,0,1:T(1,128)}), f32[1,8,1024]{2,0,1:T(1,128)S(1)}, u32[]{:S(2)}, u32[]{:S(2)}) async-start(f32[1,8,1024]{2,0,1:T(1,128)} %bitcast.27), calls=%async_computation | async-start | bytes 65536 | tf_op jit(solution)/shard_map/all_to_all | solution.py:36
Sparse Core Ops, SparseCore 0:
  9.5 22.5 all-gather.2
where the time goes:
time: 181 us; the launch traced here: 180 us
  blocking collectives  143 us (79%)
  between operations  14.7 us (8%)
  matrix products  10.4 us (6%)
  starting transfers between devices  7.3 us (4%)
  local copies, waits for them, and re-layouts  3.87 us (2%)
    psum x2, blocking collectives, divergence_rows(): kl_p, kl_q = lax.psum((part_p, part_q), 'vocab')  53.7 us
    all_gather x1, blocking collectives, local(): lax.all_gather(hid_student, 'vocab', axis=0, tiled=True)  30.7 us
    unnamed x1, blocking collectives  21.8 us
    psum x1, blocking collectives, normalizers(): mass_s, mass_t = lax.psum((local_s, local_t), 'vocab')  19 us
    pmax x1, blocking collectives, normalizers(): top_s, top_t = lax.pmax((peak_s, peak_t), 'vocab')  17.2 us
    all_to_all x1, starting transfers between devices, local(): lax.all_to_all(teacher_logits, 'vocab', split_axis=1, concat_axis=0, tile...  7.26 us
    dot_general x1, matrix products, local(): lax.dot_general(grad_logits, full_s, (((1,), (1,)), ((), ())), preferred_...  5.67 us
    dot_general x1, matrix products, local(): student = jnp.dot(all_s, full_s, preferred_element_type=jnp.float32)  4.68 us
  transfers between devices with their start and end apart: 2, of which 0 were waited for; matrix products, arithmetic and copies ran while one was open for 1% of the time, Pallas kernels for 0%

commit v1 on v0

v1 whole, which is shorter than its diff:
```python
import functools
import math

import jax
import jax.numpy as jnp
from jax import lax
from jax.experimental import pallas as pl
from jax.experimental.pallas import tpu as pltpu
from jax.sharding import PartitionSpec as P

LANES = 128


def kernel(
    nv,
    hid,
    teach,
    scale,
    head,
    loss,
    grad,
    w,
    hid_in,
    hid_f,
    part,
    rows,
    g_out,
    g_in,
    back_f,
    back,
    back_in,
    w_sems,
    send_sems,
    recv_sems,
):
    tokens = 2 * nv
    depth, cols = head.shape
    hb = depth // LANES
    vb = cols // LANES
    v = lax.axis_index("vocab")
    t = lax.axis_index("tok")
    me = 2 * v + t
    slot = t * nv + v

    chunks = 4
    step = depth // chunks

    def w_copy(c):
        part_of = pl.ds(c * step, step)
        return pltpu.make_async_copy(head.at[part_of], w.at[part_of], w_sems.at[c])

    for c in range(chunks):
        w_copy(c).start()

    def each_peer(fn):
        def one(k, _):
            peer = lax.rem(me + k, tokens)
            fn(peer, peer // 2, lax.rem(peer, 2))
            return 0

        lax.fori_loop(1, tokens, one, 0, unroll=tokens <= 16)

    barrier = pltpu.get_barrier_semaphore()

    def greet(peer, pv, pt):
        pl.semaphore_signal(barrier, inc=1, device_id={"vocab": pv, "tok": pt})

    each_peer(greet)
    pl.semaphore_wait(barrier, tokens - 1)

    def send(phase, src_of, dst):
        def one(peer, pv, pt):
            pltpu.make_async_remote_copy(
                src_ref=src_of(peer, pv, pt),
                dst_ref=dst,
                send_sem=send_sems.at[phase],
                recv_sem=recv_sems.at[phase],
                device_id={"vocab": pv, "tok": pt},
            ).start()

        each_peer(one)

    def wait(sems, phase, buf, block):
        ref = buf.at[pl.ds(0, (tokens - 1) * block)]
        pltpu.make_async_copy(ref, ref, sems.at[phase]).wait()

    def block(i, size):
        return pl.ds(pl.multiple_of(i * size, size), size)

    send(0, lambda p, pv, pt: hid.at[block(pt, hb)], hid_in.at[block(me, hb)])
    hid_in[block(me, hb), :] = hid[block(t, hb), :]

    teacher = teach[...]
    top_t = jnp.max(teacher, keepdims=True)
    logq = teacher - (top_t + jnp.log(jnp.sum(jnp.exp(teacher - top_t), keepdims=True)))

    wait(recv_sems, 0, hid_in, hb)
    hid_f[...] = hid_in[...].astype(jnp.float32)
    x = jnp.concatenate(
        [hid_f[pl.ds(r, tokens, stride=hb), :].astype(jnp.bfloat16) for r in range(hb)], axis=1
    )
    for c in range(chunks):
        w_copy(c).wait()
    wide = 2 * LANES
    for c in range(cols // wide):
        y = jnp.dot(x, w[:, c * wide : (c + 1) * wide], preferred_element_type=jnp.float32)
        for h in range(2):
            part[pl.ds(2 * c + h, tokens, stride=vb), :] = y[:, h * LANES : (h + 1) * LANES]

    send(1, lambda p, pv, pt: part.at[block(p, vb)], rows.at[block(slot, vb)])
    rows[block(slot, vb), :] = part[block(me, vb), :]
    wait(recv_sems, 1, rows, vb)
    student = rows[0 : nv * vb, :] + rows[nv * vb : 2 * nv * vb, :]

    top_s = jnp.max(student, keepdims=True)
    logp = student - (top_s + jnp.log(jnp.sum(jnp.exp(student - top_s), keepdims=True)))
    logm = (
        jnp.maximum(logp, logq)
        + jnp.log1p(jnp.exp(-jnp.abs(logp - logq)))
        + jnp.float32(math.log(0.5))
    )
    prob_p = jnp.exp(logp)
    diff_p = logp - logm
    kl_p = jnp.sum(prob_p * diff_p, keepdims=True)
    weight = scale[...].astype(jnp.float32)
    g = (weight * prob_p * 0.5 * (diff_p - kl_p)).astype(jnp.bfloat16)
    g_out[...] = g.astype(jnp.float32)

    send(2, lambda p, pv, pt: g_out.at[block(pv, vb)], g_in.at[block(me, vb)])
    g_in[block(me, vb), :] = g_out[block(v, vb), :]
    kl_q = jnp.sum(jnp.exp(logq) * (logq - logm), keepdims=True)
    loss[...] = jnp.broadcast_to(0.5 * kl_p + 0.5 * kl_q, loss.shape)

    wait(recv_sems, 2, g_in, vb)
    gl = jnp.concatenate(
        [g_in[pl.ds(j, tokens, stride=vb), :].astype(jnp.bfloat16) for j in range(vb)], axis=1
    )
    for c in range(depth // wide):
        y = lax.dot_general(
            gl,
            w[c * wide : (c + 1) * wide, :],
            (((1,), (1,)), ((), ())),
            preferred_element_type=jnp.float32,
        )
        for h in range(2):
            back_f[pl.ds(2 * c + h, tokens, stride=hb), :] = y[:, h * LANES : (h + 1) * LANES]
    back[...] = back_f[...].astype(jnp.bfloat16)

    send(3, lambda p, pv, pt: back.at[block(p, hb)], back_in.at[block(slot, hb)])
    back_in[block(slot, hb), :] = back[block(me, hb), :]
    wait(recv_sems, 3, back_in, hb)
    got = back_in[...].astype(jnp.float32).reshape(2, nv, hb, LANES)
    grad[...] = jnp.sum(got, axis=1).reshape(2 * hb, LANES).astype(grad.dtype)

    wait(send_sems, 0, hid_in, hb)
    wait(send_sems, 1, rows, vb)
    wait(send_sems, 2, g_in, vb)
    wait(send_sems, 3, back_in, hb)


def local(nv, hid_student, teacher_logits, token_scale, head_student):
    tokens = 2 * nv
    depth, cols = head_student.shape
    hb = depth // LANES
    vb = cols // LANES
    f32, bf16 = jnp.float32, jnp.bfloat16
    vmem = pl.BlockSpec(memory_space=pltpu.VMEM)
    dma = pltpu.SemaphoreType.DMA
    loss, grad = pl.pallas_call(
        functools.partial(kernel, nv),
        out_shape=(
            jax.ShapeDtypeStruct((1, LANES), f32),
            jax.ShapeDtypeStruct((2 * hb, LANES), f32),
        ),
        in_specs=[vmem, vmem, vmem, pl.BlockSpec(memory_space=pltpu.HBM)],
        out_specs=(vmem, vmem),
        scratch_shapes=[
            pltpu.VMEM((depth, cols), bf16),
            pltpu.VMEM((tokens * hb, LANES), bf16),
            pltpu.VMEM((tokens * hb, LANES), f32),
            pltpu.VMEM((tokens * vb, LANES), f32),
            pltpu.VMEM((tokens * vb, LANES), f32),
            pltpu.VMEM((nv * vb, LANES), f32),
            pltpu.VMEM((tokens * vb, LANES), f32),
            pltpu.VMEM((tokens * hb, LANES), f32),
            pltpu.VMEM((tokens * hb, LANES), bf16),
            pltpu.VMEM((tokens * hb, LANES), bf16),
            dma((4,)),
            dma((4,)),
            dma((4,)),
        ],
        compiler_params=pltpu.CompilerParams(
            collective_id=0, has_side_effects=True, vmem_limit_bytes=48 * 1024 * 1024
        ),
    )(
        hid_student.reshape(2 * hb, LANES),
        teacher_logits.reshape(nv * vb, LANES),
        token_scale.reshape(1, 1),
        head_student,
    )
    return loss[0, :1], grad.astype(bf16).reshape(1, 2 * depth)


def solution(mesh):
    in_specs = (
        P(("groups", "vocab", "tok"), None),
        P(("groups", "vocab", "tok"), None),
        P(("groups", "vocab", "tok")),
        P("tok", "vocab"),
    )
    out_specs = (P(("groups", "vocab", "tok")), P(("groups", "vocab", "tok"), None))
    return jax.shard_map(
        functools.partial(local, mesh.shape["vocab"]),
        mesh=mesh,
        in_specs=in_specs,
        out_specs=out_specs,
        check_vma=False,
    )
```

time: 181 us -> 32.5 us (0.18)
  blocking collectives: 143 us -> 0 us
  Pallas kernels: 0 us -> 25.4 us
  between operations: 14.7 us -> 2.48 us
  matrix products: 10.4 us -> 0 us
  starting transfers between devices: 7.3 us -> 0 us
    psum x3 -> x0, blocking collectives: 72.8 us -> none  [the longest x2 53.7 us: divergence_rows(): kl_p, kl_q = lax.psum((part_p, part_q), 'vocab')]
    all_gather x1 -> x0, blocking collectives: 30.7 us -> none  [local(): lax.all_gather(hid_student, 'vocab', axis=0, tiled=True)]
    pallas_call x0 -> x1, Pallas kernels: none -> 25.4 us  [local(): pl.pallas_call(functools.partial(kernel, nv), out_shape=(jax.ShapeDtypeSt...]
    unnamed x1 -> x0, blocking collectives: 21.8 us -> none
    pmax x1 -> x0, blocking collectives: 17.2 us -> none  [normalizers(): top_s, top_t = lax.pmax((peak_s, peak_t), 'vocab')]
    dot_general x2 -> x0, matrix products: 10.4 us -> none  [the longest x1 5.67 us: local(): lax.dot_general(grad_logits, full_s, (((1,), (1,)), ((), ())), preferred_...]
    all_to_all x1 -> x0, starting transfers between devices: 7.26 us -> none  [local(): lax.all_to_all(teacher_logits, 'vocab', split_axis=1, concat_axis=0, tile...]
  transfers between devices with their start and end apart: 2 -> 0, of which waited for: 0 -> 0; matrix products, arithmetic and copies ran while one was open for 1% -> 0% of each run, Pallas kernels for 0% -> 0%
where the time goes in v1:
time: 32.5 us; the launch traced here: 32.2 us
  Pallas kernels  25.4 us (78%)
  local copies, waits for them, and re-layouts  3.56 us (11%)
  between operations  2.48 us (8%)
  other arithmetic  0.77 us (2%)
    pallas_call x1, Pallas kernels, local(): pl.pallas_call(functools.partial(kernel, nv), out_shape=(jax.ShapeDtypeSt...  25.4 us
    unnamed x5, local copies, waits for them, and re-layouts  3.56 us
    unnamed x2, other arithmetic  0.77 us

profile of v1, /device:TPU:0, one launch (start us, length us, event | category | flops | bytes accessed | tf_op | source)
XLA Modules:
  0.0 32.2 jit_solution(7170610235314023801)
XLA Ops:
  1.3 0.8 %reduce = bf16[4096]{0:T(1024)(128)(2,1)S(1)} reduce(bf16[1,4096]{1,0:T(2,128)(2,1)} %param.4, bf16[]{:T(256)} %constant.3), dimensions={0}, to_apply=%param.4.reduce_sub_computation | reduce | bytes 16386 | tf_op args[0]
  2.1 0.0 copy-start
  2.1 2.2 %copy-done = bf16[2048,1024]{1,0:T(8,128)(2,1)S(1)} copy-done((bf16[2048,1024]{1,0:T(8,128)(2,1)S(1)}, bf16[2048,1024]{1,0:T(8,128)(2,1)}, u32[]{:S(2)}) %copy-start) | copy-done | bytes 4194328
  4.2 0.0 copy-start.1
  4.2 0.8 %copy-done.1 = f32[1,8192]{1,0:T(1,128)S(1)} copy-done((f32[1,8192]{1,0:T(1,128)S(1)}, f32[1,8192]{1,0:T(1,128)}, u32[]{:S(2)}) %copy-start.1) | copy-done | bytes 32792
  5.0 25.4 %shard_map.59 = (f32[1,128]{1,0:T(1,128)S(1)}, f32[32,128]{1,0:T(8,128)S(1)}) custom-call(bf16[32,128]{1,0:T(8,128)(2,1)S(1)} %bitcast.13, f32[64,128]{1,0:T(8,128)S(1)} %bitcast.12, bf16[1,1]{1,0:T(2,128)(2,1)} %bitcast.11.scale, bf16[2048,1024]{1,0:T(8,128)(2,1)S(1)} %copy-done), custom_call_target="tpu_custom_call" | custom-call | tf_op jit(solution)/shard_map/pallas_call | solution.py:169
  30.4 0.6 %copy.8 = bf16[1,1,32,128]{3,1,2,0:T(2,128)(2,1)} copy(bf16[1,1,32,128]{3,2,1,0:T(8,128)(2,1)S(1)} %convert_bitcast_fusion) | data formatting | bytes 16384
  (1 shorter events, 0.0 us)
Async XLA Ops:
  2.1 2.2 %copy-start = (bf16[2048,1024]{1,0:T(8,128)(2,1)S(1)}, bf16[2048,1024]{1,0:T(8,128)(2,1)}, u32[]{:S(2)}) copy-start(bf16[2048,1024]{1,0:T(8,128)(2,1)} %head.1) | copy-start | bytes 12582916
  4.2 0.8 %copy-start.1 = (f32[1,8192]{1,0:T(1,128)S(1)}, f32[1,8192]{1,0:T(1,128)}, u32[]{:S(2)}) copy-start(f32[1,8192]{1,0:T(1,128)} %param.5) | copy-start | bytes 98308

commit v2 on v1

--- a/solution.py
+++ b/solution.py
@@ -20,6 +20,10 @@
     loss,
     grad,
     w,
+    teach_v,
+    hid_row,
+    hid_32,
+    hid_16,
     hid_in,
     hid_f,
     part,
@@ -49,6 +53,10 @@
         part_of = pl.ds(c * step, step)
         return pltpu.make_async_copy(head.at[part_of], w.at[part_of], w_sems.at[c])
 
+    hid_copy = pltpu.make_async_copy(hid, hid_row, w_sems.at[chunks])
+    teach_copy = pltpu.make_async_copy(teach, teach_v, w_sems.at[chunks + 1])
+    hid_copy.start()
+    teach_copy.start()
     for c in range(chunks):
         w_copy(c).start()
 
@@ -66,6 +74,11 @@
         pl.semaphore_signal(barrier, inc=1, device_id={"vocab": pv, "tok": pt})
 
     each_peer(greet)
+    hid_copy.wait()
+    for r in range(2 * hb):
+        lanes = slice(r * LANES, (r + 1) * LANES)
+        hid_32[r : r + 1, :] = hid_row[:, lanes].astype(jnp.float32)
+    hid_16[...] = hid_32[...].astype(jnp.bfloat16)
     pl.semaphore_wait(barrier, tokens - 1)
 
     def send(phase, src_of, dst):
@@ -87,10 +100,11 @@
     def block(i, size):
         return pl.ds(pl.multiple_of(i * size, size), size)
 
-    send(0, lambda p, pv, pt: hid.at[block(pt, hb)], hid_in.at[block(me, hb)])
-    hid_in[block(me, hb), :] = hid[block(t, hb), :]
-
-    teacher = teach[...]
+    send(0, lambda p, pv, pt: hid_16.at[block(pt, hb)], hid_in.at[block(me, hb)])
+    hid_in[block(me, hb), :] = hid_16[block(t, hb), :]
+
+    teach_copy.wait()
+    teacher = teach_v[...]
     top_t = jnp.max(teacher, keepdims=True)
     logq = teacher - (top_t + jnp.log(jnp.sum(jnp.exp(teacher - top_t), keepdims=True)))
 
@@ -150,7 +164,9 @@
     back_in[block(slot, hb), :] = back[block(me, hb), :]
     wait(recv_sems, 3, back_in, hb)
     got = back_in[...].astype(jnp.float32).reshape(2, nv, hb, LANES)
-    grad[...] = jnp.sum(got, axis=1).reshape(2 * hb, LANES).astype(grad.dtype)
+    hid_32[...] = jnp.sum(got, axis=1).reshape(2 * hb, LANES)
+    for r in range(2 * hb):
+        grad[:, r * LANES : (r + 1) * LANES] = hid_32[r : r + 1, :].astype(grad.dtype)
 
     wait(send_sems, 0, hid_in, hb)
     wait(send_sems, 1, rows, vb)
@@ -165,17 +181,22 @@
     vb = cols // LANES
     f32, bf16 = jnp.float32, jnp.bfloat16
     vmem = pl.BlockSpec(memory_space=pltpu.VMEM)
+    hbm = pl.BlockSpec(memory_space=pltpu.HBM)
     dma = pltpu.SemaphoreType.DMA
     loss, grad = pl.pallas_call(
         functools.partial(kernel, nv),
         out_shape=(
             jax.ShapeDtypeStruct((1, LANES), f32),
-            jax.ShapeDtypeStruct((2 * hb, LANES), f32),
+            jax.ShapeDtypeStruct((1, 2 * depth), bf16),
         ),
-        in_specs=[vmem, vmem, vmem, pl.BlockSpec(memory_space=pltpu.HBM)],
+        in_specs=[hbm, hbm, vmem, hbm],
         out_specs=(vmem, vmem),
         scratch_shapes=[
             pltpu.VMEM((depth, cols), bf16),
+            pltpu.VMEM((nv * vb, LANES), f32),
+            pltpu.VMEM((1, 2 * depth), bf16),
+            pltpu.VMEM((2 * hb, LANES), f32),
+            pltpu.VMEM((2 * hb, LANES), bf16),
             pltpu.VMEM((tokens * hb, LANES), bf16),
             pltpu.VMEM((tokens * hb, LANES), f32),
             pltpu.VMEM((tokens * vb, LANES), f32),
@@ -185,20 +206,20 @@
             pltpu.VMEM((tokens * hb, LANES), f32),
             pltpu.VMEM((tokens * hb, LANES), bf16),
             pltpu.VMEM((tokens * hb, LANES), bf16),
-            dma((4,)),
+            dma((6,)),
             dma((4,)),
             dma((4,)),
         ],
         compiler_params=pltpu.CompilerParams(
-            collective_id=0, has_side_effects=True, vmem_limit_bytes=48 * 1024 * 1024
+            collective_id=0, has_side_effects=True, vmem_limit_bytes=60 * 1024 * 1024
         ),
     )(
-        hid_student.reshape(2 * hb, LANES),
+        hid_student,
         teacher_logits.reshape(nv * vb, LANES),
         token_scale.reshape(1, 1),
         head_student,
     )
-    return loss[0, :1], grad.astype(bf16).reshape(1, 2 * depth)
+    return loss[0, :1], grad
 
 
 def solution(mesh):

time: 32.5 us -> 30.6 us (0.942)
  local copies, waits for them, and re-layouts: 3.56 us -> 1.34 us
  other arithmetic: 0.77 us -> 0 us
  between operations: 2.48 us -> 3.05 us
  Pallas kernels: 25.4 us -> 25.8 us
    unnamed x5 -> x1, local copies, waits for them, and re-layouts: 3.56 us -> 1.34 us
    unnamed x2 -> x0, other arithmetic: 0.77 us -> none
    pallas_call x1, Pallas kernels: 25.4 us -> 25.8 us  [local(): pl.pallas_call(functools.partial(kernel, nv), out_shape=(jax.ShapeDtypeSt...]
where the time goes in v2:
time: 30.6 us; the launch traced here: 30.2 us
  Pallas kernels  25.8 us (84%)
  between operations  3.05 us (10%)
  local copies, waits for them, and re-layouts  1.34 us (4%)
    pallas_call x1, Pallas kernels, local(): pl.pallas_call(functools.partial(kernel, nv), out_shape=(jax.ShapeDtypeSt...  25.8 us
    unnamed x1, local copies, waits for them, and re-layouts  1.34 us

profile of v2, /device:TPU:0, one launch (start us, length us, event | category | flops | bytes accessed | tf_op | source)
XLA Modules:
  0.0 30.2 jit_solution(11957577556069319187)
XLA Ops:
  1.3 25.8 %shard_map.59 = (f32[1,128]{1,0:T(1,128)}, bf16[1,4096]{1,0:T(2,128)(2,1)}) custom-call(bf16[1,4096]{1,0:T(2,128)(2,1)} %hid.1, f32[64,128]{1,0:T(8,128)} %bitcast.5, bf16[1,1]{1,0:T(2,128)(2,1)} %bitcast.4.scale, bf16[2048,1024]{1,0:T(8,128)(2,1)} %head.1), custom_call_target="tpu_custom_call" | custom-call | tf_op jit(solution)/shard_map/pallas_call | solution.py:186
  27.7 1.3 %copy.10 = bf16[1,4096]{1,0:T(2,128)(2,1)} copy(bf16[1,4096]{1,0:T(2,128)(2,1)} %get-tuple-element.9) | data formatting | bytes 16384

commit v3 on v2

--- a/solution.py
+++ b/solution.py
@@ -26,14 +26,19 @@
     hid_16,
     hid_in,
     hid_f,
+    logq_v,
+    logq_in,
     part,
-    rows,
-    g_out,
-    g_in,
+    other,
+    norm_out,
+    norm_in,
     back_f,
     back,
     back_in,
+    stat,
+    stat_in,
     w_sems,
+    tok_sems,
     send_sems,
     recv_sems,
 ):
@@ -46,6 +51,7 @@
     me = 2 * v + t
     slot = t * nv + v
 
+    wide = 2 * LANES
     chunks = 4
     step = depth // chunks
 
@@ -79,6 +85,12 @@
         lanes = slice(r * LANES, (r + 1) * LANES)
         hid_32[r : r + 1, :] = hid_row[:, lanes].astype(jnp.float32)
     hid_16[...] = hid_32[...].astype(jnp.bfloat16)
+    teach_copy.wait()
+    teacher = teach_v[...]
+    top_t = jnp.max(teacher, keepdims=True)
+    logq_v[...] = teacher - (
+        top_t + jnp.log(jnp.sum(jnp.exp(teacher - top_t), keepdims=True))
+    )
     pl.semaphore_wait(barrier, tokens - 1)
 
     def send(phase, src_of, dst):
@@ -100,13 +112,20 @@
     def block(i, size):
         return pl.ds(pl.multiple_of(i * size, size), size)
 
+    def tok_copy(c):
+        part_of = pl.ds(c * wide, wide)
+        return pltpu.make_async_remote_copy(
+            src_ref=part.at[:, part_of],
+            dst_ref=other.at[:, part_of],
+            send_sem=tok_sems.at[0, c],
+            recv_sem=tok_sems.at[1, c],
+            device_id={"tok": 1 - t},
+        )
+
     send(0, lambda p, pv, pt: hid_16.at[block(pt, hb)], hid_in.at[block(me, hb)])
+    send(1, lambda p, pv, pt: logq_v.at[block(pv, vb)], logq_in.at[block(me, vb)])
     hid_in[block(me, hb), :] = hid_16[block(t, hb), :]
-
-    teach_copy.wait()
-    teacher = teach_v[...]
-    top_t = jnp.max(teacher, keepdims=True)
-    logq = teacher - (top_t + jnp.log(jnp.sum(jnp.exp(teacher - top_t), keepdims=True)))
+    logq_in[block(me, vb), :] = logq_v[block(v, vb), :]
 
     wait(recv_sems, 0, hid_in, hb)
     hid_f[...] = hid_in[...].astype(jnp.float32)
@@ -115,19 +134,42 @@
     )
     for c in range(chunks):
         w_copy(c).wait()
-    wide = 2 * LANES
     for c in range(cols // wide):
-        y = jnp.dot(x, w[:, c * wide : (c + 1) * wide], preferred_element_type=jnp.float32)
-        for h in range(2):
-            part[pl.ds(2 * c + h, tokens, stride=vb), :] = y[:, h * LANES : (h + 1) * LANES]
-
-    send(1, lambda p, pv, pt: part.at[block(p, vb)], rows.at[block(slot, vb)])
-    rows[block(slot, vb), :] = part[block(me, vb), :]
-    wait(recv_sems, 1, rows, vb)
-    student = rows[0 : nv * vb, :] + rows[nv * vb : 2 * nv * vb, :]
-
-    top_s = jnp.max(student, keepdims=True)
-    logp = student - (top_s + jnp.log(jnp.sum(jnp.exp(student - top_s), keepdims=True)))
+        part[:, c * wide : (c + 1) * wide] = jnp.dot(
+            x, w[:, c * wide : (c + 1) * wide], preferred_element_type=jnp.float32
+        )
+        tok_copy(c).start()
+
+    wait(recv_sems, 1, logq_in, vb)
+    logq = jnp.concatenate([logq_in[pl.ds(j, tokens, stride=vb), :] for j in range(vb)], axis=1)
+    for c in range(cols // wide):
+        tok_copy(c).wait_recv()
+    student = part[...] + other[...]
+
+    top = jnp.max(student, axis=1, keepdims=True)
+    norm = top + jnp.log(jnp.sum(jnp.exp(student - top), axis=1, keepdims=True))
+    norm_out[...] = jnp.broadcast_to(norm, norm_out.shape)
+
+    def send_norm(k, _):
+        pv = lax.rem(v + k, nv)
+        pltpu.make_async_remote_copy(
+            src_ref=norm_out,
+            dst_ref=norm_in.at[block(v, tokens)],
+            send_sem=send_sems.at[2],
+            recv_sem=recv_sems.at[2],
+            device_id={"vocab": pv},
+        ).start()
+        return 0
+
+    lax.fori_loop(1, nv, send_norm, 0, unroll=nv <= 8)
+    norm_in[block(v, tokens), :] = norm_out[...]
+    norms_ref = norm_in.at[pl.ds(0, (nv - 1) * tokens)]
+    pltpu.make_async_copy(norms_ref, norms_ref, recv_sems.at[2]).wait()
+    norms = norm_in[...].reshape(nv, tokens, LANES)
+    peak = jnp.max(norms, axis=0)
+    norm_all = peak + jnp.log(jnp.sum(jnp.exp(norms - peak[None]), axis=0))
+
+    logp = student - norm_all[:, 0:1]
     logm = (
         jnp.maximum(logp, logq)
         + jnp.log1p(jnp.exp(-jnp.abs(logp - logq)))
@@ -135,43 +177,61 @@
     )
     prob_p = jnp.exp(logp)
     diff_p = logp - logm
-    kl_p = jnp.sum(prob_p * diff_p, keepdims=True)
-    weight = scale[...].astype(jnp.float32)
-    g = (weight * prob_p * 0.5 * (diff_p - kl_p)).astype(jnp.bfloat16)
-    g_out[...] = g.astype(jnp.float32)
-
-    send(2, lambda p, pv, pt: g_out.at[block(pv, vb)], g_in.at[block(me, vb)])
-    g_in[block(me, vb), :] = g_out[block(v, vb), :]
-    kl_q = jnp.sum(jnp.exp(logq) * (logq - logm), keepdims=True)
-    loss[...] = jnp.broadcast_to(0.5 * kl_p + 0.5 * kl_q, loss.shape)
-
-    wait(recv_sems, 2, g_in, vb)
-    gl = jnp.concatenate(
-        [g_in[pl.ds(j, tokens, stride=vb), :].astype(jnp.bfloat16) for j in range(vb)], axis=1
-    )
+    part_p = jnp.sum(prob_p * diff_p, axis=1, keepdims=True)
+    mass = jnp.sum(prob_p, axis=1, keepdims=True)
+    centre = part_p / jnp.maximum(mass, 1e-30)
+    main = prob_p * (diff_p - centre)
+    high = main.astype(jnp.bfloat16)
+    low = (main - high.astype(jnp.float32)).astype(jnp.bfloat16)
+    left = jnp.concatenate([high, low, prob_p.astype(jnp.bfloat16)], axis=0)
     for c in range(depth // wide):
         y = lax.dot_general(
-            gl,
+            left,
             w[c * wide : (c + 1) * wide, :],
             (((1,), (1,)), ((), ())),
             preferred_element_type=jnp.float32,
         )
+        moved = y[0:tokens] + y[tokens : 2 * tokens]
+        mean = y[2 * tokens :]
         for h in range(2):
-            back_f[pl.ds(2 * c + h, tokens, stride=hb), :] = y[:, h * LANES : (h + 1) * LANES]
+            lanes = slice(h * LANES, (h + 1) * LANES)
+            back_f[pl.ds(2 * c + h, tokens, stride=2 * hb), :] = moved[:, lanes]
+            back_f[pl.ds(hb + 2 * c + h, tokens, stride=2 * hb), :] = mean[:, lanes]
     back[...] = back_f[...].astype(jnp.bfloat16)
 
-    send(3, lambda p, pv, pt: back.at[block(p, hb)], back_in.at[block(slot, hb)])
-    back_in[block(slot, hb), :] = back[block(me, hb), :]
-    wait(recv_sems, 3, back_in, hb)
-    got = back_in[...].astype(jnp.float32).reshape(2, nv, hb, LANES)
-    hid_32[...] = jnp.sum(got, axis=1).reshape(2 * hb, LANES)
+    part_q = jnp.sum(jnp.exp(logq) * (logq - logm), axis=1, keepdims=True)
+    for r, column in enumerate((part_p, part_q, centre, centre)):
+        stat[pl.ds(r, tokens, stride=8), :] = jnp.broadcast_to(column, (tokens, LANES))
+
+    send(3, lambda p, pv, pt: back.at[block(p, 2 * hb)], back_in.at[block(slot, 2 * hb)])
+
+    def four(i):
+        return pl.ds(pl.multiple_of(i * 8, 8), 4)
+
+    send(4, lambda p, pv, pt: stat.at[four(p)], stat_in.at[four(slot)])
+    back_in[block(slot, 2 * hb), :] = back[block(me, 2 * hb), :]
+    stat_in[four(slot), :] = stat[four(me), :]
+    wait(recv_sems, 4, stat_in, 4)
+    kl_p = jnp.sum(stat_in[pl.ds(0, tokens, stride=8), :][:nv], axis=0, keepdims=True)
+    kl_q = jnp.sum(stat_in[pl.ds(1, tokens, stride=8), :][:nv], axis=0, keepdims=True)
+    loss[...] = 0.5 * kl_p + 0.5 * kl_q
+    shift = (kl_p - stat_in[pl.ds(2, tokens, stride=8), :]).reshape(tokens, 1, LANES)
+    weight = 0.5 * scale[...].astype(jnp.float32)
+
+    wait(recv_sems, 3, back_in, 2 * hb)
+    got = back_in[...].astype(jnp.float32).reshape(tokens, 2, hb, LANES)
+    terms = (got[:, 0] - shift * got[:, 1]).reshape(2, nv, hb, LANES)
+    hid_32[...] = weight * jnp.sum(terms, axis=1).reshape(2 * hb, LANES)
     for r in range(2 * hb):
         grad[:, r * LANES : (r + 1) * LANES] = hid_32[r : r + 1, :].astype(grad.dtype)
 
     wait(send_sems, 0, hid_in, hb)
-    wait(send_sems, 1, rows, vb)
-    wait(send_sems, 2, g_in, vb)
-    wait(send_sems, 3, back_in, hb)
+    wait(send_sems, 1, logq_in, vb)
+    for c in range(cols // wide):
+        tok_copy(c).wait_send()
+    pltpu.make_async_copy(norms_ref, norms_ref, send_sems.at[2]).wait()
+    wait(send_sems, 3, back_in, 2 * hb)
+    wait(send_sems, 4, stat_in, 4)
 
 
 def local(nv, hid_student, teacher_logits, token_scale, head_student):
@@ -199,16 +259,21 @@
             pltpu.VMEM((2 * hb, LANES), bf16),
             pltpu.VMEM((tokens * hb, LANES), bf16),
             pltpu.VMEM((tokens * hb, LANES), f32),
-            pltpu.VMEM((tokens * vb, LANES), f32),
-            pltpu.VMEM((tokens * vb, LANES), f32),
             pltpu.VMEM((nv * vb, LANES), f32),
             pltpu.VMEM((tokens * vb, LANES), f32),
-            pltpu.VMEM((tokens * hb, LANES), f32),
-            pltpu.VMEM((tokens * hb, LANES), bf16),
-            pltpu.VMEM((tokens * hb, LANES), bf16),
+            pltpu.VMEM((tokens, cols), f32),
+            pltpu.VMEM((tokens, cols), f32),
+            pltpu.VMEM((tokens, LANES), f32),
+            pltpu.VMEM((nv * tokens, LANES), f32),
+            pltpu.VMEM((tokens * 2 * hb, LANES), f32),
+            pltpu.VMEM((tokens * 2 * hb, LANES), bf16),
+            pltpu.VMEM((tokens * 2 * hb, LANES), bf16),
+            pltpu.VMEM((tokens * 8, LANES), f32),
+            pltpu.VMEM((tokens * 8, LANES), f32),
             dma((6,)),
-            dma((4,)),
-            dma((4,)),
+            dma((2, cols // (2 * LANES))),
+            dma((5,)),
+            dma((5,)),
         ],
         compiler_params=pltpu.CompilerParams(
             collective_id=0, has_side_effects=True, vmem_limit_bytes=60 * 1024 * 1024

time: 30.6 us -> 29.9 us (0.977)
  Pallas kernels: 25.8 us -> 25.2 us
    pallas_call x1, Pallas kernels: 25.8 us -> 25.2 us  [local(): pl.pallas_call(functools.partial(kernel, nv), out_shape=(jax.ShapeDtypeSt...]
where the time goes in v3:
time: 29.9 us; the launch traced here: 29.5 us
  Pallas kernels  25.2 us (84%)
  between operations  3.05 us (10%)
  local copies, waits for them, and re-layouts  1.34 us (4%)
    pallas_call x1, Pallas kernels, local(): pl.pallas_call(functools.partial(kernel, nv), out_shape=(jax.ShapeDtypeSt...  25.2 us
    unnamed x1, local copies, waits for them, and re-layouts  1.34 us

profile of v3, /device:TPU:0, one launch (start us, length us, event | category | flops | bytes accessed | tf_op | source)
XLA Modules:
  0.0 29.5 jit_solution(7422790627792794758)
XLA Ops:
  1.3 25.2 %shard_map.59 = (f32[1,128]{1,0:T(1,128)}, bf16[1,4096]{1,0:T(2,128)(2,1)}) custom-call(bf16[1,4096]{1,0:T(2,128)(2,1)} %hid.1, f32[64,128]{1,0:T(8,128)} %bitcast.5, bf16[1,1]{1,0:T(2,128)(2,1)} %bitcast.4.scale, bf16[2048,1024]{1,0:T(8,128)(2,1)} %head.1), custom_call_target="tpu_custom_call" | custom-call | tf_op jit(solution)/shard_map/pallas_call | solution.py:246
  27.1 1.3 %copy.10 = bf16[1,4096]{1,0:T(2,128)(2,1)} copy(bf16[1,4096]{1,0:T(2,128)(2,1)} %get-tuple-element.9) | data formatting | bytes 16384

commit v4 on v3

--- a/solution.py
+++ b/solution.py
@@ -67,12 +67,14 @@
         w_copy(c).start()
 
     def each_peer(fn):
-        def one(k, _):
-            peer = lax.rem(me + k, tokens)
+        def one(base, k):
+            peer = base + lax.rem(me + k, nv)
             fn(peer, peer // 2, lax.rem(peer, 2))
-            return 0
-
-        lax.fori_loop(1, tokens, one, 0, unroll=tokens <= 16)
+            return base
+
+        near = me // nv * nv
+        lax.fori_loop(0, nv, lambda k, b: one(b, k), nv - near, unroll=nv <= 8)
+        lax.fori_loop(1, nv, lambda k, b: one(b, k), near, unroll=nv <= 8)
 
     barrier = pltpu.get_barrier_semaphore()
 
@@ -123,7 +125,6 @@
         )
 
     send(0, lambda p, pv, pt: hid_16.at[block(pt, hb)], hid_in.at[block(me, hb)])
-    send(1, lambda p, pv, pt: logq_v.at[block(pv, vb)], logq_in.at[block(me, vb)])
     hid_in[block(me, hb), :] = hid_16[block(t, hb), :]
     logq_in[block(me, vb), :] = logq_v[block(v, vb), :]
 
@@ -139,9 +140,8 @@
             x, w[:, c * wide : (c + 1) * wide], preferred_element_type=jnp.float32
         )
         tok_copy(c).start()
-
-    wait(recv_sems, 1, logq_in, vb)
-    logq = jnp.concatenate([logq_in[pl.ds(j, tokens, stride=vb), :] for j in range(vb)], axis=1)
+    send(1, lambda p, pv, pt: logq_v.at[block(pv, vb)], logq_in.at[block(me, vb)])
+
     for c in range(cols // wide):
         tok_copy(c).wait_recv()
     student = part[...] + other[...]
@@ -150,8 +150,8 @@
     norm = top + jnp.log(jnp.sum(jnp.exp(student - top), axis=1, keepdims=True))
     norm_out[...] = jnp.broadcast_to(norm, norm_out.shape)
 
-    def send_norm(k, _):
-        pv = lax.rem(v + k, nv)
+    def send_norm(base, k):
+        pv = base + lax.rem(v + k, half)
         pltpu.make_async_remote_copy(
             src_ref=norm_out,
             dst_ref=norm_in.at[block(v, tokens)],
@@ -159,10 +159,15 @@
             recv_sem=recv_sems.at[2],
             device_id={"vocab": pv},
         ).start()
-        return 0
-
-    lax.fori_loop(1, nv, send_norm, 0, unroll=nv <= 8)
+        return base
+
+    half = nv // 2
+    close = v // half * half
+    lax.fori_loop(0, half, lambda k, b: send_norm(b, k), half - close, unroll=nv <= 8)
+    lax.fori_loop(1, half, lambda k, b: send_norm(b, k), close, unroll=nv <= 8)
     norm_in[block(v, tokens), :] = norm_out[...]
+    wait(recv_sems, 1, logq_in, vb)
+    logq = jnp.concatenate([logq_in[pl.ds(j, tokens, stride=vb), :] for j in range(vb)], axis=1)
     norms_ref = norm_in.at[pl.ds(0, (nv - 1) * tokens)]
     pltpu.make_async_copy(norms_ref, norms_ref, recv_sems.at[2]).wait()
     norms = norm_in[...].reshape(nv, tokens, LANES)
@@ -180,6 +185,16 @@
     part_p = jnp.sum(prob_p * diff_p, axis=1, keepdims=True)
     mass = jnp.sum(prob_p, axis=1, keepdims=True)
     centre = part_p / jnp.maximum(mass, 1e-30)
+    part_q = jnp.sum(jnp.exp(logq) * (logq - logm), axis=1, keepdims=True)
+    for r, column in enumerate((part_p, part_q, centre, centre)):
+        stat[pl.ds(r, tokens, stride=8), :] = jnp.broadcast_to(column, (tokens, LANES))
+
+    def four(i):
+        return pl.ds(pl.multiple_of(i * 8, 8), 4)
+
+    send(4, lambda p, pv, pt: stat.at[four(p)], stat_in.at[four(slot)])
+    stat_in[four(slot), :] = stat[four(me), :]
+
     main = prob_p * (diff_p - centre)
     high = main.astype(jnp.bfloat16)
     low = (main - high.astype(jnp.float32)).astype(jnp.bfloat16)
@@ -199,18 +214,9 @@
             back_f[pl.ds(hb + 2 * c + h, tokens, stride=2 * hb), :] = mean[:, lanes]
     back[...] = back_f[...].astype(jnp.bfloat16)
 
-    part_q = jnp.sum(jnp.exp(logq) * (logq - logm), axis=1, keepdims=True)
-    for r, column in enumerate((part_p, part_q, centre, centre)):
-        stat[pl.ds(r, tokens, stride=8), :] = jnp.broadcast_to(column, (tokens, LANES))
-
     send(3, lambda p, pv, pt: back.at[block(p, 2 * hb)], back_in.at[block(slot, 2 * hb)])
 
-    def four(i):
-        return pl.ds(pl.multiple_of(i * 8, 8), 4)
-
-    send(4, lambda p, pv, pt: stat.at[four(p)], stat_in.at[four(slot)])
     back_in[block(slot, 2 * hb), :] = back[block(me, 2 * hb), :]
-    stat_in[four(slot), :] = stat[four(me), :]
     wait(recv_sems, 4, stat_in, 4)
     kl_p = jnp.sum(stat_in[pl.ds(0, tokens, stride=8), :][:nv], axis=0, keepdims=True)
     kl_q = jnp.sum(stat_in[pl.ds(1, tokens, stride=8), :][:nv], axis=0, keepdims=True)

time: 29.9 us -> 28.9 us (0.967)
  Pallas kernels: 25.2 us -> 24.1 us
    pallas_call x1, Pallas kernels: 25.2 us -> 24.1 us  [local(): pl.pallas_call(functools.partial(kernel, nv), out_shape=(jax.ShapeDtypeSt...]
where the time goes in v4:
time: 28.9 us; the launch traced here: 28.5 us
  Pallas kernels  24.1 us (83%)
  between operations  3.05 us (11%)
  local copies, waits for them, and re-layouts  1.34 us (5%)
    pallas_call x1, Pallas kernels, local(): pl.pallas_call(functools.partial(kernel, nv), out_shape=(jax.ShapeDtypeSt...  24.1 us
    unnamed x1, local copies, waits for them, and re-layouts  1.34 us

profile of v4, /device:TPU:0, one launch (start us, length us, event | category | flops | bytes accessed | tf_op | source)
XLA Modules:
  0.0 28.5 jit_solution(15047497240976357305)
XLA Ops:
  1.3 24.1 %shard_map.59 = (f32[1,128]{1,0:T(1,128)}, bf16[1,4096]{1,0:T(2,128)(2,1)}) custom-call(bf16[1,4096]{1,0:T(2,128)(2,1)} %hid.1, f32[64,128]{1,0:T(8,128)} %bitcast.5, bf16[1,1]{1,0:T(2,128)(2,1)} %bitcast.4.scale, bf16[2048,1024]{1,0:T(8,128)(2,1)} %head.1), custom_call_target="tpu_custom_call" | custom-call | tf_op jit(solution)/shard_map/pallas_call | solution.py:252
  26.1 1.3 %copy.10 = bf16[1,4096]{1,0:T(2,128)(2,1)} copy(bf16[1,4096]{1,0:T(2,128)(2,1)} %get-tuple-element.9) | data formatting | bytes 16384

commit v5 on v4

--- a/solution.py
+++ b/solution.py
@@ -199,6 +199,20 @@
     high = main.astype(jnp.bfloat16)
     low = (main - high.astype(jnp.float32)).astype(jnp.bfloat16)
     left = jnp.concatenate([high, low, prob_p.astype(jnp.bfloat16)], axis=0)
+    hh = hb // 2
+    region = tokens * hb
+
+    def send_back(part_no):
+        def rows_of(i):
+            return pl.ds(pl.multiple_of(part_no * region + i * hb, hb), hb)
+
+        back[part_no * region : (part_no + 1) * region, :] = back_f[
+            part_no * region : (part_no + 1) * region, :
+        ].astype(jnp.bfloat16)
+        phase = 3 + 2 * part_no
+        send(phase, lambda p, pv, pt: back.at[rows_of(p)], back_in.at[rows_of(slot)])
+        back_in[rows_of(slot), :] = back[rows_of(me), :]
+
     for c in range(depth // wide):
         y = lax.dot_general(
             left,
@@ -210,13 +224,13 @@
         mean = y[2 * tokens :]
         for h in range(2):
             lanes = slice(h * LANES, (h + 1) * LANES)
-            back_f[pl.ds(2 * c + h, tokens, stride=2 * hb), :] = moved[:, lanes]
-            back_f[pl.ds(hb + 2 * c + h, tokens, stride=2 * hb), :] = mean[:, lanes]
-    back[...] = back_f[...].astype(jnp.bfloat16)
-
-    send(3, lambda p, pv, pt: back.at[block(p, 2 * hb)], back_in.at[block(slot, 2 * hb)])
-
-    back_in[block(slot, 2 * hb), :] = back[block(me, 2 * hb), :]
+            part_no, pos = divmod(2 * c + h, hh)
+            row = part_no * region + pos
+            back_f[pl.ds(row, tokens, stride=hb), :] = moved[:, lanes]
+            back_f[pl.ds(row + hh, tokens, stride=hb), :] = mean[:, lanes]
+        if (2 * c + 2) % hh == 0:
+            send_back((2 * c + 1) // hh)
+
     wait(recv_sems, 4, stat_in, 4)
     kl_p = jnp.sum(stat_in[pl.ds(0, tokens, stride=8), :][:nv], axis=0, keepdims=True)
     kl_q = jnp.sum(stat_in[pl.ds(1, tokens, stride=8), :][:nv], axis=0, keepdims=True)
@@ -224,10 +238,14 @@
     shift = (kl_p - stat_in[pl.ds(2, tokens, stride=8), :]).reshape(tokens, 1, LANES)
     weight = 0.5 * scale[...].astype(jnp.float32)
 
-    wait(recv_sems, 3, back_in, 2 * hb)
-    got = back_in[...].astype(jnp.float32).reshape(tokens, 2, hb, LANES)
-    terms = (got[:, 0] - shift * got[:, 1]).reshape(2, nv, hb, LANES)
-    hid_32[...] = weight * jnp.sum(terms, axis=1).reshape(2 * hb, LANES)
+    for part_no in range(2):
+        wait(recv_sems, 3 + 2 * part_no, back_in, hb)
+        got = back_in[part_no * region : (part_no + 1) * region, :].astype(jnp.float32)
+        got = got.reshape(tokens, 2, hh, LANES)
+        terms = (got[:, 0] - shift * got[:, 1]).reshape(2, nv, hh, LANES)
+        total = weight * jnp.sum(terms, axis=1)
+        for r in range(2):
+            hid_32[r * hb + part_no * hh : r * hb + (part_no + 1) * hh, :] = total[r]
     for r in range(2 * hb):
         grad[:, r * LANES : (r + 1) * LANES] = hid_32[r : r + 1, :].astype(grad.dtype)
 
@@ -236,7 +254,8 @@
     for c in range(cols // wide):
         tok_copy(c).wait_send()
     pltpu.make_async_copy(norms_ref, norms_ref, send_sems.at[2]).wait()
-    wait(send_sems, 3, back_in, 2 * hb)
+    wait(send_sems, 3, back_in, hb)
+    wait(send_sems, 5, back_in, hb)
     wait(send_sems, 4, stat_in, 4)
 
 
@@ -278,8 +297,8 @@
             pltpu.VMEM((tokens * 8, LANES), f32),
             dma((6,)),
             dma((2, cols // (2 * LANES))),
-            dma((5,)),
-            dma((5,)),
+            dma((6,)),
+            dma((6,)),
         ],
         compiler_params=pltpu.CompilerParams(
             collective_id=0, has_side_effects=True, vmem_limit_bytes=60 * 1024 * 1024

time: 28.9 us -> 28.6 us (0.990)
  Pallas kernels: 24.1 us -> 23.8 us
    pallas_call x1, Pallas kernels: 24.1 us -> 23.8 us  [local(): pl.pallas_call(functools.partial(kernel, nv), out_shape=(jax.ShapeDtypeSt...]
where the time goes in v5:
time: 28.6 us; the launch traced here: 28.2 us
  Pallas kernels  23.8 us (83%)
  between operations  3.05 us (11%)
  local copies, waits for them, and re-layouts  1.34 us (5%)
    pallas_call x1, Pallas kernels, local(): pl.pallas_call(functools.partial(kernel, nv), out_shape=(jax.ShapeDtypeSt...  23.8 us
    unnamed x1, local copies, waits for them, and re-layouts  1.34 us

profile of v5, /device:TPU:0, one launch (start us, length us, event | category | flops | bytes accessed | tf_op | source)
XLA Modules:
  0.0 28.2 jit_solution(15019157353349783973)
XLA Ops:
  1.3 23.8 %shard_map.59 = (f32[1,128]{1,0:T(1,128)}, bf16[1,4096]{1,0:T(2,128)(2,1)}) custom-call(bf16[1,4096]{1,0:T(2,128)(2,1)} %hid.1, f32[64,128]{1,0:T(8,128)} %bitcast.5, bf16[1,1]{1,0:T(2,128)(2,1)} %bitcast.4.scale, bf16[2048,1024]{1,0:T(8,128)(2,1)} %head.1), custom_call_target="tpu_custom_call" | custom-call | tf_op jit(solution)/shard_map/pallas_call | solution.py:271
  25.7 1.3 %copy.10 = bf16[1,4096]{1,0:T(2,128)(2,1)} copy(bf16[1,4096]{1,0:T(2,128)(2,1)} %get-tuple-element.9) | data formatting | bytes 16384
